TPU v7x, 32 devices: a whole 2x2x4 slice. The times are simulated.
32 devices in a mesh: groups: 2 (over y), tensor: 4 (over z), expert: 4 (over x, core).
Axes of the slice: x: 2, y: 2, z: 4, core: 2. Of those that a mesh axis runs over, the one named last changes fastest.
Arguments:
- hidden_in: bfloat16 [64, 4096], P(('groups', 'expert'), 'tensor'), parts along dimension 0, may hold values from -6 to 6
- queries: bfloat16 [64, 4096], P(('groups', 'expert')), parts along dimension 0, may hold values from -140 to 140
- cache_keys: bfloat16 [64, 1024, 512], P(('groups', 'expert'), 'tensor'), parts along dimension 0, may hold values from -4 to 4
- cache_values: bfloat16 [64, 1024, 512], P(('groups', 'expert'), 'tensor'), parts along dimension 0, may hold values from -6 to 6
- new_key: bfloat16 [64, 512], P(('groups', 'expert')), parts along dimension 0, may hold values from -6 to 6
- new_value: bfloat16 [64, 512], P(('groups', 'expert')), parts along dimension 0, may hold values from -6 to 6
- cache_lengths: int32 [64], P(('groups', 'expert')), parts along dimension 0, may hold values from 2 to 1024, as said below
- out_weight: bfloat16 [4096, 4096], P('tensor'), may hold values from -2 to 2
- norm_gain: bfloat16 [4096], P('tensor'), may hold values from 0.5 to 1.5
- gate_probs: float32 [64, 8], P(('groups', 'expert')), parts along dimension 0, may hold values from 0.05 to 1
- expert_ids: int32 [64, 8], P(('groups', 'expert')), parts along dimension 0, may hold values from 0 to 63, all different within a row; in each aligned block of 8 rows (0 to 7, 8 to 15, ...) at most 2 rows name the same one
- gate_up: bfloat16 [64, 4096, 1536], P('expert', 'tensor'), may hold values from -0.09375 to 0.09375
- down_proj: bfloat16 [64, 768, 4096], P('expert', None, 'tensor'), may hold values from -0.21875 to 0.21875
Outputs:
- mixed: bfloat16 [64, 4096], P(('groups', 'expert'), 'tensor'), parts along dimension 0
There are 2 independent parts, one for each index of `groups`. A program takes and returns all parts, laid end to end along the dimension named above; an argument that names none is the same for every part. Nothing has to cross between parts.
Inputs may be any that keep to these rules, and one draw needn't show every extreme that they name: Positions below cache_lengths[r] of row r are live; some row has 1024 live positions. `expert_ids`: each row names 8 different experts; among the rows of one index of expert (aligned blocks of 8 rows) no expert is named more than 2 times, and in some block one expert is named exactly 2 times.
All inputs are finite; a program needn't handle non-finite values.
Results may differ from a plain program's by a relative error of at most 0.023.
Values may be sent and summed in bfloat16 or wider, within the bound.
A program may use at most 192 MiB of HBM per device.

v0:
```python
import math

import jax
import jax.numpy as jnp
from jax import lax
from jax.sharding import PartitionSpec as P

HD = 128
KV = 4
MOST = 2


neg_large = -1e30


def body(
    hidden_in,
    queries,
    cache_keys,
    cache_values,
    new_key,
    new_value,
    cache_lengths,
    out_weight,
    norm_gain,
    gate_probs,
    expert_ids,
    gate_up,
    down_proj,
):
    row_count = queries.shape[0]
    head_count = queries.shape[1] // HD
    group_size = head_count // KV
    local_length = cache_keys.shape[1]
    score_scale = 1.0 / math.sqrt(HD)
    tensor_pos = lax.axis_index("tensor")
    tensor_count = lax.axis_size("tensor")
    my_heads = head_count // tensor_count
    query_heads = queries.reshape(row_count, KV, group_size, HD)
    key_heads = cache_keys.reshape(row_count, local_length, KV, HD)
    value_heads = cache_values.reshape(row_count, local_length, KV, HD)
    scores = (
        jnp.einsum("rkgd,rpkd->rkgp", query_heads, key_heads, preferred_element_type=jnp.float32)
        * score_scale
    )
    position = tensor_pos * local_length + jnp.arange(local_length, dtype=jnp.int32)
    live_mask = (position[None, :] < cache_lengths[:, None])[:, None, None, :]
    local_high = jnp.max(jnp.where(live_mask, scores, neg_large), axis=3)
    own_score = (
        jnp.einsum(
            "rkgd,rkd->rkg",
            query_heads,
            new_key.reshape(row_count, KV, HD),
            preferred_element_type=jnp.float32,
        )
        * score_scale
    )
    own_mine = lax.dynamic_slice_in_dim(
        own_score.reshape(row_count, head_count), tensor_pos * my_heads, my_heads, 1
    )
    global_high = lax.pmax(local_high, "tensor")
    highest = jnp.maximum(global_high, own_score)
    weights = jnp.where(live_mask, jnp.exp(scores - highest[..., None]), 0.0)
    weight_totals = jnp.sum(weights, axis=3).reshape(row_count, head_count)
    value_sums = jnp.einsum(
        "rkgp,rpkd->rkgd",
        weights.astype(jnp.bfloat16),
        value_heads,
        preferred_element_type=jnp.float32,
    )
    value_sums = value_sums.reshape(row_count, head_count * HD)
    head_values, head_totals = (
        lax.psum_scatter(
            value_sums.astype(jnp.bfloat16), "tensor", scatter_dimension=1, tiled=True
        ).astype(jnp.float32),
        lax.psum_scatter(
            weight_totals.astype(jnp.bfloat16), "tensor", scatter_dimension=1, tiled=True
        ).astype(jnp.float32),
    )
    highest_mine = lax.dynamic_slice_in_dim(
        highest.reshape(row_count, head_count), tensor_pos * my_heads, my_heads, 1
    )
    own_weight = jnp.exp(own_mine - highest_mine)
    own_values = jnp.broadcast_to(
        new_value.reshape(row_count, KV, 1, HD), (row_count, KV, group_size, HD)
    )
    own_values = own_values.reshape(row_count, head_count * HD)
    own_values = lax.dynamic_slice_in_dim(own_values, tensor_pos * my_heads * HD, my_heads * HD, 1)
    own_values = own_values.reshape(row_count, my_heads, HD).astype(jnp.float32)
    low_own = lax.optimization_barrier(own_weight.astype(jnp.bfloat16)).astype(jnp.float32)
    numerator = head_values.reshape(row_count, my_heads, HD) + low_own[..., None] * own_values
    attended = (numerator / (head_totals + own_weight)[..., None]).astype(jnp.bfloat16)
    attended = attended.reshape(row_count, my_heads * HD)
    proj_term = jnp.dot(attended, out_weight, preferred_element_type=jnp.float32)
    proj_sum = lax.psum_scatter(
        proj_term.astype(jnp.bfloat16), "tensor", scatter_dimension=1, tiled=True
    ).astype(jnp.float32)
    residual = (hidden_in.astype(jnp.float32) + proj_sum).astype(jnp.bfloat16)
    wide = residual.astype(jnp.float32)
    feature_total = residual.shape[1] * tensor_count
    full = lax.all_gather(residual, "tensor", axis=1, tiled=True).astype(jnp.float32)
    mean_square = jnp.sum(full * full, axis=1) / feature_total
    normed = (
        wide * lax.rsqrt(mean_square + 1e-06)[:, None] * norm_gain.astype(jnp.float32)[None, :]
    ).astype(jnp.bfloat16)
    feat_width = normed.shape[1]
    exp_local = gate_up.shape[0]
    hidden_units = down_proj.shape[1]
    owner_count = lax.axis_size("expert")
    top_count = expert_ids.shape[1]
    expert_total = exp_local * owner_count
    slot_total = expert_total * MOST
    flat_ids = expert_ids.reshape(row_count * top_count)
    matches = (flat_ids[:, None] == jnp.arange(expert_total, dtype=jnp.int32)[None, :]).astype(
        jnp.int32
    )
    earlier = jnp.cumsum(matches, axis=0) - matches
    slot_rank = jnp.sum(earlier * matches, axis=1)
    column = flat_ids % exp_local * (owner_count * MOST) + flat_ids // exp_local * MOST + slot_rank
    placing = (column[:, None] == jnp.arange(slot_total, dtype=jnp.int32)[None, :]).astype(
        jnp.bfloat16
    )
    copies = jnp.broadcast_to(normed[:, None, :], (row_count, top_count, feat_width)).reshape(
        row_count * top_count, feat_width
    )
    outgoing = jnp.einsum("pc,pd->cd", placing, copies, preferred_element_type=jnp.float32).astype(
        jnp.bfloat16
    )
    outgoing = outgoing.reshape(exp_local, owner_count, MOST, feat_width)
    arrived = lax.all_to_all(outgoing, "expert", split_axis=1, concat_axis=1, tiled=True)
    slot_count = arrived.shape[2]
    slot_rows = arrived.reshape(exp_local, owner_count * slot_count, feat_width)
    pre_term = jnp.einsum("erd,edf->erf", slot_rows, gate_up, preferred_element_type=jnp.float32)
    summed = lax.psum(pre_term.astype(jnp.bfloat16), "tensor").astype(jnp.float32)
    hidden = (jax.nn.silu(summed[..., :hidden_units]) * summed[..., hidden_units:]).astype(
        jnp.bfloat16
    )
    result = jnp.einsum(
        "erf,efd->erd", hidden, down_proj, preferred_element_type=jnp.float32
    ).astype(jnp.bfloat16)
    result = result.reshape(exp_local, owner_count, slot_count, feat_width)
    returned = lax.all_to_all(result, "expert", split_axis=1, concat_axis=1, tiled=True)
    pair_out = jnp.dot(
        placing, returned.reshape(slot_total, feat_width), preferred_element_type=jnp.float32
    )
    pair_out = pair_out.reshape(row_count, top_count, feat_width)
    mixture = jnp.einsum("rk,rkd->rd", gate_probs, pair_out)
    return (wide + mixture).astype(jnp.bfloat16)


def solution(mesh):
    return jax.shard_map(
        body,
        mesh=mesh,
        in_specs=(
            P(("groups", "expert"), "tensor"),
            P(("groups", "expert"), None),
            P(("groups", "expert"), "tensor", None),
            P(("groups", "expert"), "tensor", None),
            P(("groups", "expert"), None),
            P(("groups", "expert"), None),
            P(("groups", "expert")),
            P("tensor", None),
            P("tensor"),
            P(("groups", "expert"), None),
            P(("groups", "expert"), None),
            P("expert", "tensor", None),
            P("expert", None, "tensor"),
        ),
        out_specs=P(("groups", "expert"), "tensor"),
        check_vma=False,
    )
```

profile of v0, /device:TPU:0, one launch (start us, length us, event | category | flops | bytes accessed | tf_op | source)
XLA Modules:
  0.0 182.0 jit_solution(239529710955013688)
XLA Ops:
  6.6 0.9 broadcast_compare_fusion
  7.4 0.7 copy-done
  8.1 1.6 select_reduce_fusion
  9.8 20.6 %pmax.7 = f32[8,4,8]{2,1,0:T(4,128)S(1)} all-reduce(f32[8,4,8]{2,1,0:T(4,128)S(1)} %get-tuple-element.9), channel_id=1, replica_groups=mesh['groups'=2,'tensor'=4,'expert'=4] {'tensor'}, use_global_device_ids=true, to_apply=%region_1.2 | all-reduce | flops 256 | bytes 2048 | tf_op jit(solution)/shard_map/pmax | solution.py:61
  30.4 0.2 fusion.29
  30.6 2.0 %fusion.15 = bf16[1,8,32,128]{3,2,1,0:T(8,128)(2,1)S(1)} fusion(f32[8,4,8,256]{3,2,1,0:T(8,128)S(1)} %get-tuple-element.10, f32[8,4,8]{2,1,0:T(4,128)S(1)} %get-tuple-element.6, pred[8,256]{1,0:T(8,128)(4,1)S(1)} %broadcast_compare_fusion, bf16[8,256,512]{2,1,0:T(8,128)(2,1)} %param.16), kind=kOutput, calls=%fused_computation.14 | convolution fusion | flops 17006592 | bytes 2427904 | tf_op jit(solution)/shard_map/rkgp,rpkd->rkgd/dot_general | solution.py:65
  32.6 0.7 copy.68
  33.3 0.0 reduce-scatter.6.cloned.1.call-start
  33.3 0.2 fusion.19
  33.5 0.1 reshape.170
  33.6 0.1 convert_element_type.90
  33.7 8.4 %all-reduce = bf16[8,32]{1,0:T(8,128)(2,1)S(1)} all-reduce(bf16[8,32]{1,0:T(8,128)(2,1)S(1)} %convert_element_type.90), channel_id=3, replica_groups=mesh['groups'=2,'tensor'=4,'expert'=4] {'tensor'}, use_global_device_ids=true, to_apply=%region_4.5.clone | all-reduce | flops 256 | bytes 1024
  42.1 0.1 reshape.169
  42.1 0.1 eq.52
  42.2 0.1 fusion.37
  42.3 0.6 dynamic-slice
  43.6 0.1 fusion.57
  43.6 0.1 copy.27
  43.7 0.1 copy.28
  43.8 0.1 reduce_window_sum.11
  43.9 0.2 select_reduce_fusion.1
  44.1 6.5 %reduce-scatter.4.cloned.1.call-done = bf16[8,1024]{1,0:T(8,128)(2,1)} async-done(((bf16[8,4096]{1,0:T(8,128)(2,1)}), bf16[8,1024]{1,0:T(8,128)(2,1)}) %reduce-scatter.4.cloned.1.call-update) | async-done | bytes 16400 | tf_op jit(solution)/shard_map/reduce_scatter | solution.py:73
  50.6 5.3 %convolution_convert_fusion = bf16[8,4096]{1,0:T(8,128)(2,1)} fusion(bf16[1024,4096]{1,0:T(8,128)(2,1)} %param.20, bf16[8,1024]{1,0:T(8,128)(2,1)} %reduce-scatter.4.cloned.1.call-done, f32[8,8]{0,1:T(8,128)S(1)} %copy.28, bf16[8,4096]{1,0:T(8,128)(2,1)S(1)} %bitcast.70, s32[]{:T(128)S(6)} %select_n.43, f32[8,8]{0,1:T(8,128)S(1)} %copy.27), kind=kOutput, calls=%fused_computation | convolution fusion | flops 67190784 | bytes 8495108 | tf_op jit(solution)/shard_map/dot_general | solution.py:94
  55.9 0.0 all-reduce.3.cloned.1.call-start
  56.0 17.3 %reduce-scatter.6.cloned.1.call-done = bf16[8,1024]{1,0:T(8,128)(2,1)} async-done(((bf16[8,4096]{1,0:T(8,128)(2,1)}), bf16[8,1024]{1,0:T(8,128)(2,1)}) %reduce-scatter.6.cloned.1.call-update) | async-done | bytes 16400 | tf_op jit(solution)/shard_map/reduce_scatter | solution.py:95
  73.3 0.7 add_convert_fusion
  74.0 13.1 %all_gather.3 = bf16[8,4096]{1,0:T(8,128)(2,1)S(1)} all-gather(bf16[8,1024]{1,0:T(8,128)(2,1)S(1)} %add_convert_fusion), channel_id=1, replica_groups=mesh['groups'=2,'tensor'=4,'expert'=4] {'tensor'}, dimensions={1}, use_global_device_ids=true | all-gather | bytes 81920 | tf_op jit(solution)/shard_map/all_gather | solution.py:101
  87.1 0.1 multiply_reduce_fusion
  87.3 0.1 fusion.33
  87.4 0.3 convolution_convert_fusion.2
  87.7 0.1 reshape.173
  87.8 0.2 copy.29
  88.0 8.6 %all_to_all.10 = bf16[16,4,2,1024]{3,2,0,1:T(2,128)(2,1)S(1)} all-to-all(bf16[16,4,2,1024]{3,2,0,1:T(2,128)(2,1)S(1)} %copy.29), channel_id=1, replica_groups=mesh['groups'=2,'tensor'=4,'expert'=4] {'expert'}, dimensions={1} | all-to-all | bytes 524288 | tf_op jit(solution)/shard_map/all_to_all | solution.py:130
  96.6 0.2 copy.30
  96.8 0.1 reshape.174
  97.0 19.5 %convolution_convert_fusion.1 = bf16[16,8,1536]{2,1,0:T(8,128)(2,1)} fusion(bf16[16,8,1024]{2,1,0:T(8,128)(2,1)S(1)} %reshape.174, bf16[16,1024,1536]{2,1,0:T(8,128)(2,1)} %param.24), kind=kOutput, calls=%fused_computation.1 | convolution fusion | flops 402849792 | bytes 50987008 | tf_op jit(solution)/shard_map/erd,edf->erf/dot_general | solution.py:133
  116.4 0.1 reduce_sum.31
  116.5 34.4 %all-reduce.3.cloned.1.call-done = bf16[16,8,1536]{2,1,0:T(8,128)(2,1)} async-done(((bf16[16,8,1536]{2,1,0:T(8,128)(2,1)}), bf16[16,8,1536]{2,1,0:T(8,128)(2,1)}) %all-reduce.3.cloned.1.call-update) | async-done | bytes 393232 | tf_op jit(solution)/shard_map/psum | solution.py:134
  150.9 1.1 convert_element_type.103
  152.0 11.7 %convolution_convert_fusion.3 = bf16[16,8,1024]{2,1,0:T(8,128)(2,1)S(1)} fusion(bf16[16,768,1024]{2,1,0:T(8,128)(2,1)} %param.25, f32[16,8,1536]{2,1,0:T(8,128)S(1)} %convert_element_type.103), kind=kOutput, calls=%fused_computation.9 | convolution fusion | flops 202047488 | bytes 26214400 | tf_op jit(solution)/shard_map/erf,efd->erd/dot_general | solution.py:138
  163.7 0.1 reshape.175
  163.8 0.9 copy.31
  164.7 3.4 %all-to-all-start.1 = ((bf16[16,4,2,1024]{3,2,0,1:T(2,128)(2,1)}), bf16[16,4,2,1024]{3,2,0,1:T(2,128)(2,1)S(1)}, u32[]{:S(2)}, u32[]{:S(2)}) async-start(bf16[16,4,2,1024]{3,2,0,1:T(2,128)(2,1)} %copy.31), calls=%async_computation.3 | async-start | bytes 524288 | tf_op jit(solution)/shard_map/all_to_all | solution.py:142
  168.1 6.0 %all-to-all-done.1 = bf16[16,4,2,1024]{3,2,0,1:T(2,128)(2,1)S(1)} async-done(((bf16[16,4,2,1024]{3,2,0,1:T(2,128)(2,1)}), bf16[16,4,2,1024]{3,2,0,1:T(2,128)(2,1)S(1)}, u32[]{:S(2)}, u32[]{:S(2)}) %all-to-all-start.1) | async-done | bytes 262176 | tf_op jit(solution)/shard_map/all_to_all | solution.py:142
  174.1 0.2 copy.32
  174.3 0.1 reshape.179
  174.5 0.4 fusion.9
  174.8 0.6 fusion.34
  (30 shorter events, 0.2 us)
Async XLA Ops:
  6.5 1.6 copy-start
  6.5 23.8 %copy-start.2 = (bf16[8,4096]{1,0:T(8,128)(2,1)S(1)}, bf16[8,4096]{1,0:T(8,128)(2,1)}, u32[]{:S(2)}) copy-start(bf16[8,4096]{1,0:T(8,128)(2,1)} %param.14) | copy-start | bytes 196612
  6.5 23.8 %copy-start.8 = (bf16[8,512]{1,0:T(8,128)(2,1)S(1)}, bf16[8,512]{1,0:T(8,128)(2,1)}, u32[]{:S(2)}) copy-start(bf16[8,512]{1,0:T(8,128)(2,1)} %param.17) | copy-start | bytes 24580
  6.5 44.1 %reduce-scatter.4.cloned.1.call-start = ((), (), s32[]{:S(2)}) async-start(), calls=%async_computation.4 | async-start | bytes 81920 | tf_op jit(solution)/shard_map/reduce_scatter | solution.py:73
  9.7 32.4 %copy-start.4 = (s32[8,8]{1,0:T(8,128)S(1)}, s32[8,8]{1,0:T(8,128)}, u32[]{:S(2)}) copy-start(s32[8,8]{1,0:T(8,128)} %param.23) | copy-start | bytes 772
  9.7 32.6 %copy-start.9 = (u32[32]{0:T(128)S(1)}, u32[32]{0:T(128)}, u32[]{:S(2)}) copy-start(u32[32]{0:T(128)} %constant.71) | copy-start | bytes 388
  9.7 34.1 %copy-start.7 = (bf16[1024]{0:T(1024)(128)(2,1)S(1)}, bf16[1024]{0:T(1024)(128)(2,1)}, u32[]{:S(2)}) copy-start(bf16[1024]{0:T(1024)(128)(2,1)} %param.21) | copy-start | bytes 6148
  9.7 40.9 %copy-start.5 = (bf16[8,512]{1,0:T(8,128)(2,1)S(1)}, bf16[8,512]{1,0:T(8,128)(2,1)}, u32[]{:S(2)}) copy-start(bf16[8,512]{1,0:T(8,128)(2,1)} %param.18) | copy-start | bytes 24580
  33.3 40.0 %reduce-scatter.6.cloned.1.call-start = ((), (), s32[]{:S(2)}) async-start(), calls=%async_computation.5 | async-start | bytes 81920 | tf_op jit(solution)/shard_map/reduce_scatter | solution.py:95
  50.6 22.7 %copy-start.3 = (bf16[8,1024]{1,0:T(8,128)(2,1)S(1)}, bf16[8,1024]{1,0:T(8,128)(2,1)}, u32[]{:S(2)}) copy-start(bf16[8,1024]{1,0:T(8,128)(2,1)} %param.13) | copy-start | bytes 49156
  55.9 95.0 %all-reduce.3.cloned.1.call-start = ((), (), s32[]{:S(2)}) async-start(), calls=%async_computation.6 | async-start | bytes 786432 | tf_op jit(solution)/shard_map/psum | solution.py:134
  152.0 23.5 %copy-start.1 = (bf16[8,256,512]{2,1,0:T(8,128)(2,1)S(1)}, bf16[8,256,512]{2,1,0:T(8,128)(2,1)}, u32[]{:S(2)}) copy-start(bf16[8,256,512]{2,1,0:T(8,128)(2,1)} %param.15) | copy-start | bytes 6291460
  163.7 10.8 %copy-start.6 = (f32[8,8]{1,0:T(8,128)S(1)}, f32[8,8]{1,0:T(8,128)}, u32[]{:S(2)}) copy-start(f32[8,8]{1,0:T(8,128)} %param.22) | copy-start | bytes 772
  164.7 9.4 %all-to-all-start.1 = ((bf16[16,4,2,1024]{3,2,0,1:T(2,128)(2,1)}), bf16[16,4,2,1024]{3,2,0,1:T(2,128)(2,1)S(1)}, u32[]{:S(2)}, u32[]{:S(2)}) async-start(bf16[16,4,2,1024]{3,2,0,1:T(2,128)(2,1)} %copy.31), calls=%async_computation.3 | async-start | bytes 524288 | tf_op jit(solution)/shard_map/all_to_all | solution.py:142
Sparse Core Ops, SparseCore 0:
  33.4 17.1 reduce-scatter.3
  56.0 17.2 reduce-scatter.5
  116.6 34.3 all-reduce.2
where the time goes:
time: 183 us; the launch traced here: 182 us
  waiting for transfers between devices  64.3 us (35%)
  blocking collectives  50.7 us (28%)
  matrix products  40.9 us (22%)
  between operations  14 us (8%)
  local copies, waits for them, and re-layouts  4.5 us (2%)
  other arithmetic  4.21 us (2%)
  starting transfers between devices  3.49 us (2%)
    psum x1, waiting for transfers between devices, body(): lax.psum(pre_term.astype(jnp.bfloat16), 'tensor').astype(jnp.float32)  34.4 us
    pmax x1, blocking collectives, body(): global_high = lax.pmax(local_high, 'tensor')  20.6 us
    dot_general x1, matrix products, body(): jnp.einsum('erd,edf->erf', slot_rows, gate_up, preferred_element_type=jnp...  19.5 us
    reduce_scatter x1, waiting for transfers between devices, body(): lax.psum_scatter(proj_term.astype(jnp.bfloat16), 'tensor', scatter_dimens...  17.3 us
    all_gather x1, blocking collectives, body(): lax.all_gather(residual, 'tensor', axis=1, tiled=True).astype(jnp.float32)  13.1 us
    dot_general x1, matrix products, body(): jnp.einsum('erf,efd->erd', hidden, down_proj, preferred_element_type=jnp....  11.7 us
    all_to_all x1, blocking collectives, body(): lax.all_to_all(outgoing, 'expert', split_axis=1, concat_axis=1, tiled=True)  8.57 us
    unnamed x1, blocking collectives  8.35 us
  transfers between devices with their start and end apart: 4, of which 4 were waited for; matrix products, arithmetic and copies ran while one was open for 1% of the time, Pallas kernels for 0%

commit v1 on v0

--- a/solution.py
+++ b/solution.py
@@ -1,8 +1,11 @@
+import functools
 import math
 
 import jax
 import jax.numpy as jnp
 from jax import lax
+from jax.experimental import pallas as pl
+from jax.experimental.pallas import tpu as pltpu
 from jax.sharding import PartitionSpec as P
 
 HD = 128
@@ -148,9 +151,608 @@
     return (wide + mixture).astype(jnp.bfloat16)
 
 
+def fused_kernel(
+    tensor_count,
+    owner_count,
+    hidden_ref,
+    query_ref,
+    new_key_ref,
+    new_value_ref,
+    length_ref,
+    gain_ref,
+    prob_ref,
+    id_ref,
+    key_hbm,
+    value_hbm,
+    proj_hbm,
+    gate_hbm,
+    down_hbm,
+    out_ref,
+    key_buf,
+    value_buf,
+    proj_buf,
+    gate_buf,
+    down_buf,
+    part_high,
+    part_total,
+    part_value,
+    stat_all,
+    value_all,
+    term_all,
+    info_all,
+    rows_all,
+    square_all,
+    square_sum,
+    slot_rows,
+    slot_scale,
+    pre_mine,
+    pre_got,
+    hidden_all,
+    result_all,
+    mix_mine,
+    mix_got,
+    load_sem,
+    gate_sem,
+    down_sem,
+    send_sem,
+    recv_sem,
+    pre_send,
+    pre_recv,
+    hid_send,
+    hid_recv,
+):
+    rows, width = hidden_ref.shape
+    kv_count, group_size = query_ref.shape[1], query_ref.shape[2]
+    local_length = key_hbm.shape[1]
+    units = down_hbm.shape[1]
+    experts = gate_hbm.shape[0]
+    half = width // 2
+    pairs = experts // 2
+    per_owner = pairs // tensor_count
+    slots = owner_count * MOST
+    gate_slots, down_slots = gate_buf.shape[0], down_buf.shape[0]
+    score_scale = 1.0 / math.sqrt(HD)
+    t_me = lax.axis_index("tensor")
+    e_me = lax.axis_index("expert")
+
+    def t_at(d):
+        return lax.rem(t_me + d + tensor_count, tensor_count)
+
+    def e_at(d):
+        return lax.rem(e_me + d + owner_count, owner_count)
+
+    def gate_pair(i):
+        return t_at(1 + lax.rem(i, tensor_count)) * per_owner + i // tensor_count
+
+    def down_pair(i):
+        return t_at(lax.rem(i, tensor_count)) * per_owner + i // tensor_count
+
+    def gate_copy(i):
+        slot = lax.rem(i, gate_slots)
+        return pltpu.make_async_copy(
+            gate_hbm.at[pl.ds(gate_pair(i) * 2, 2)], gate_buf.at[slot], gate_sem.at[slot]
+        )
+
+    def down_copy(i):
+        slot = lax.rem(i, down_slots)
+        return pltpu.make_async_copy(
+            down_hbm.at[pl.ds(down_pair(i) * 2, 2)], down_buf.at[slot], down_sem.at[slot]
+        )
+
+    def remote(axis, d, kind, src, dst):
+        peer = t_at(d) if axis == "tensor" else e_at(d)
+        return pltpu.make_async_remote_copy(
+            src_ref=src,
+            dst_ref=dst,
+            send_sem=send_sem.at[kind, d - 1],
+            recv_sem=recv_sem.at[kind, d - 1],
+            device_id={axis: peer},
+            device_id_type=pl.DeviceIdType.MESH,
+        )
+
+    t_offsets = range(1, tensor_count)
+    e_offsets = range(1, owner_count)
+
+    key_copy = pltpu.make_async_copy(key_hbm, key_buf, load_sem.at[0])
+    value_copy = pltpu.make_async_copy(value_hbm, value_buf, load_sem.at[1])
+    proj_copy = pltpu.make_async_copy(proj_hbm, proj_buf, load_sem.at[2])
+    key_copy.start()
+    value_copy.start()
+    proj_copy.start()
+
+    barrier = pltpu.get_barrier_semaphore()
+    for d in t_offsets:
+        pl.semaphore_signal(
+            barrier, inc=1, device_id={"tensor": t_at(d)}, device_id_type=pl.DeviceIdType.MESH
+        )
+    for d in e_offsets:
+        pl.semaphore_signal(
+            barrier, inc=1, device_id={"expert": e_at(d)}, device_id_type=pl.DeviceIdType.MESH
+        )
+
+    lane = lax.broadcasted_iota(jnp.int32, (rows, 128), 1)
+    row = lax.broadcasted_iota(jnp.int32, (rows, 128), 0)
+    named = jnp.zeros((rows, 128), jnp.float32)
+    count = jnp.zeros((rows, 128), jnp.float32)
+    for k in range(id_ref.shape[1]):
+        hit = id_ref[:, k : k + 1] == lane // MOST
+        named = named + jnp.where(hit, prob_ref[:, k : k + 1], 0.0)
+        count = count + jnp.where(hit, 1.0, 0.0)
+    earlier = jnp.zeros((rows, 128), jnp.float32)
+    for j in range(rows):
+        earlier = earlier + jnp.where(row > j, count[j : j + 1, :], 0.0)
+    info_all[e_me] = jnp.where(earlier == (lane % MOST).astype(jnp.float32), named, 0.0)
+
+    key_copy.wait()
+    value_copy.wait()
+    for i in range(gate_slots):
+        gate_copy(i).start()
+    for i in range(down_slots):
+        down_copy(i).start()
+
+    pl.semaphore_wait(barrier, len(t_offsets) + len(e_offsets))
+    info_sends = [remote("expert", d, 0, info_all.at[e_me], info_all.at[e_me]) for d in e_offsets]
+    for copy in info_sends:
+        copy.start()
+
+    position = t_me * local_length + lax.broadcasted_iota(
+        jnp.int32, (kv_count * group_size, local_length), 1
+    )
+    for r in range(rows):
+        live = position < length_ref[r : r + 1, 0:1]
+        scores = jnp.concatenate(
+            [
+                lax.dot_general(
+                    query_ref[r, v],
+                    key_buf[r, :, v * HD : (v + 1) * HD],
+                    (((1,), (1,)), ((), ())),
+                    preferred_element_type=jnp.float32,
+                )
+                for v in range(kv_count)
+            ],
+            axis=0,
+        )
+        scores = jnp.where(live, scores * score_scale, neg_large)
+        high = jnp.max(scores, axis=1, keepdims=True)
+        weights = jnp.where(live, jnp.exp(scores - high), 0.0)
+        total = jnp.sum(weights, axis=1, keepdims=True)
+        low = weights.astype(jnp.bfloat16)
+        for v in range(kv_count):
+            span = slice(v * group_size, (v + 1) * group_size)
+            at = slice(r * group_size, (r + 1) * group_size)
+            part_value[v, at, :] = jnp.dot(
+                low[span],
+                value_buf[r, :, v * HD : (v + 1) * HD],
+                preferred_element_type=jnp.float32,
+            )
+            part_high[v, at, :] = jnp.broadcast_to(high[span], (group_size, HD))
+            part_total[v, at, :] = jnp.broadcast_to(total[span], (group_size, HD))
+
+    heads = rows * group_size
+    square = lax.broadcasted_iota(jnp.int32, (heads, 128), 0) == lax.broadcasted_iota(
+        jnp.int32, (heads, 128), 1
+    )
+    for v in range(kv_count):
+        value_all[v] = part_value[v].astype(jnp.bfloat16)
+        high_row = jnp.sum(jnp.where(square, part_high[v], 0.0), axis=0, keepdims=True)
+        total_row = jnp.sum(jnp.where(square, part_total[v], 0.0), axis=0, keepdims=True)
+        stat_all[v] = jnp.concatenate(
+            [high_row, total_row, jnp.zeros((6, 128), jnp.float32)], axis=0
+        )
+    part_sends = []
+    for d in t_offsets:
+        dest = t_at(d)
+        part_sends.append(
+            remote("tensor", d, 1, value_all.at[dest], value_all.at[kv_count + t_me])
+        )
+        part_sends.append(remote("tensor", d, 2, stat_all.at[dest], stat_all.at[kv_count + t_me]))
+    for copy in part_sends:
+        copy.start()
+
+    mine = t_me * HD
+    own_key = new_key_ref[:, pl.ds(pl.multiple_of(mine, HD), HD)].astype(jnp.float32)
+    own_value = new_value_ref[:, pl.ds(pl.multiple_of(mine, HD), HD)].astype(jnp.float32)
+
+    def spread(block):
+        wide_block = jnp.broadcast_to(block[:, None, :], (rows, group_size, HD))
+        return wide_block.reshape(heads, HD)
+
+    my_query = query_ref[:, t_me].astype(jnp.float32).reshape(heads, HD)
+    own_score = jnp.sum(my_query * spread(own_key), axis=1, keepdims=True) * score_scale
+    for copy in part_sends:
+        copy.wait_recv()
+    highs, totals, values = [], [], []
+    for s in range(tensor_count):
+        at = jnp.where(s == 0, t_me, kv_count + t_at(-s))
+        stats = stat_all[at]
+        highs.append(
+            jnp.sum(
+                jnp.where(square, jnp.broadcast_to(stats[0:1], (heads, 128)), 0.0),
+                axis=1,
+                keepdims=True,
+            )
+        )
+        totals.append(
+            jnp.sum(
+                jnp.where(square, jnp.broadcast_to(stats[1:2], (heads, 128)), 0.0),
+                axis=1,
+                keepdims=True,
+            )
+        )
+        values.append(value_all[at].astype(jnp.float32))
+    highest = own_score
+    for high in highs:
+        highest = jnp.maximum(highest, high)
+    own_weight = jnp.exp(own_score - highest)
+    total = own_weight
+    numerator = own_weight.astype(jnp.bfloat16).astype(jnp.float32) * spread(own_value)
+    for high, part, value in zip(highs, totals, values):
+        factor = jnp.exp(high - highest)
+        total = total + factor * part
+        numerator = numerator + factor * value
+    attended = (numerator / total).astype(jnp.bfloat16)
+    to_row = lax.broadcasted_iota(jnp.int32, (heads, heads), 0)
+    from_row = lax.broadcasted_iota(jnp.int32, (heads, heads), 1)
+    swap = (from_row == (to_row % rows) * group_size + to_row // rows).astype(jnp.bfloat16)
+    by_head = jnp.dot(swap, attended, preferred_element_type=jnp.float32)
+    attended = jnp.concatenate(
+        [by_head[h * rows : (h + 1) * rows] for h in range(group_size)], axis=1
+    ).astype(jnp.bfloat16)
+
+    proj_copy.wait()
+
+    def stack(block):
+        return jnp.concatenate([block[:, :half], block[:, half:]], axis=0).astype(jnp.bfloat16)
+
+    def unstack(block):
+        block = block.astype(jnp.float32)
+        return jnp.concatenate([block[:rows], block[rows:]], axis=1)
+
+    term_sends = []
+    for d in list(t_offsets) + [tensor_count]:
+        dest = t_at(d % tensor_count)
+        term = jnp.dot(
+            attended,
+            proj_buf[:, pl.ds(pl.multiple_of(dest * width, width), width)],
+            preferred_element_type=jnp.float32,
+        )
+        if d < tensor_count:
+            term_all[tensor_count + d] = stack(term)
+            copy = remote(
+                "tensor", d, 3, term_all.at[tensor_count + d], term_all.at[t_me]
+            )
+            copy.start()
+            term_sends.append(copy)
+        else:
+            term_all[t_me] = stack(term)
+    for copy in term_sends:
+        copy.wait_recv()
+    proj_sum = unstack(term_all[0])
+    for s in range(1, tensor_count):
+        proj_sum = proj_sum + unstack(term_all[s])
+    residual = (hidden_ref[...].astype(jnp.float32) + proj_sum).astype(jnp.bfloat16)
+    wide = residual.astype(jnp.float32)
+    rows_all[e_me] = stack(wide * gain_ref[...].astype(jnp.float32))
+    square_all[e_me] = jnp.broadcast_to(
+        jnp.sum(wide * wide, axis=1, keepdims=True), (rows, 128)
+    )
+    row_sends = []
+    for d in e_offsets:
+        row_sends.append(remote("expert", d, 4, rows_all.at[e_me], rows_all.at[e_me]))
+        row_sends.append(remote("expert", d, 5, square_all.at[e_me], square_all.at[e_me]))
+    for copy in row_sends:
+        copy.start()
+
+    for copy in info_sends:
+        copy.wait_recv()
+    all_rows = owner_count * rows
+    slot_total = experts * slots
+    info = jnp.concatenate([info_all[b] for b in range(owner_count)], axis=0)
+
+    def picker(shape, slot_dim):
+        slot = lax.broadcasted_iota(jnp.int32, shape, slot_dim)
+        other = lax.broadcasted_iota(jnp.int32, shape, 1 - slot_dim)
+        wanted = e_me * (experts * MOST) + (slot // slots) * MOST + slot % MOST
+        return jnp.where(other == wanted, 1.0, 0.0)
+
+    def same_block(shape, slot_dim):
+        slot = lax.broadcasted_iota(jnp.int32, shape, slot_dim)
+        other = lax.broadcasted_iota(jnp.int32, shape, 1 - slot_dim)
+        return (slot // MOST) % owner_count == other // rows
+
+    by_slot = lax.dot_general(
+        picker((slot_total, 128), 0),
+        info,
+        (((1,), (1,)), ((), ())),
+        precision=lax.Precision.HIGHEST,
+        preferred_element_type=jnp.float32,
+    )
+    placing = jnp.where(same_block((slot_total, all_rows), 0) & (by_slot > 0.0), 1.0, 0.0)
+    by_row = lax.dot_general(
+        info,
+        picker((slot_total, 128), 0),
+        (((1,), (1,)), ((), ())),
+        precision=lax.Precision.HIGHEST,
+        preferred_element_type=jnp.float32,
+    )
+    by_row = jnp.where(same_block((all_rows, slot_total), 1), by_row, 0.0)
+    gate_high = by_row.astype(jnp.bfloat16)
+    gate_low = (by_row - gate_high.astype(jnp.float32)).astype(jnp.bfloat16)
+
+    for copy in row_sends:
+        copy.wait_recv()
+    gathered = jnp.concatenate([unstack(rows_all[b]) for b in range(owner_count)], axis=0)
+    slot_rows[...] = jnp.dot(
+        placing.astype(jnp.bfloat16),
+        gathered.astype(jnp.bfloat16),
+        preferred_element_type=jnp.float32,
+    ).astype(jnp.bfloat16)
+    square_sum[t_me] = jnp.concatenate([square_all[b] for b in range(owner_count)], axis=0)
+    square_sends = [
+        remote("tensor", d, 6, square_sum.at[t_me], square_sum.at[t_me]) for d in t_offsets
+    ]
+    for copy in square_sends:
+        copy.start()
+
+    def pre_copy(i):
+        d, k = lax.rem(i, tensor_count), i // tensor_count
+        return pltpu.make_async_remote_copy(
+            src_ref=pre_mine.at[i],
+            dst_ref=pre_got.at[k, d],
+            send_sem=pre_send.at[k, d],
+            recv_sem=pre_recv.at[k, d],
+            device_id={"tensor": t_at(1 + d)},
+            device_id_type=pl.DeviceIdType.MESH,
+        )
+
+    def hid_copy(k, d):
+        pair = t_me * per_owner + k
+        return pltpu.make_async_remote_copy(
+            src_ref=hidden_all.at[pair],
+            dst_ref=hidden_all.at[pair],
+            send_sem=hid_send.at[k, d - 1],
+            recv_sem=hid_recv.at[k, d - 1],
+            device_id={"tensor": t_at(d)},
+            device_id_type=pl.DeviceIdType.MESH,
+        )
+
+    def reduce_pair(k):
+        own = k * tensor_count + tensor_count - 1
+        total = pre_mine[own].astype(jnp.float32)
+        for d in range(tensor_count - 1):
+            pre_copy(k * tensor_count + d).wait_recv()
+            total = total + pre_got[k, d].astype(jnp.float32)
+        pair = t_me * per_owner + k
+        scale = slot_scale[pl.ds(pl.multiple_of(pair * 2 * slots, 2 * slots), 2 * slots), 0:1]
+        total = total * scale
+        gate, up = total[:, :units], total[:, units:]
+        hidden_all[pair] = (gate / (1.0 + jnp.exp(-gate)) * up).astype(jnp.bfloat16)
+        for d in t_offsets:
+            hid_copy(k, d).start()
+
+    lag = 2
+
+    def gate_step(i, carry):
+        pair = gate_pair(i)
+        slot = lax.rem(i, gate_slots)
+        gate_copy(i).wait()
+        block = slot_rows[pl.ds(pl.multiple_of(pair * 2 * slots, 2 * slots), 2 * slots), :]
+        first = jnp.dot(block, gate_buf[slot, 0], preferred_element_type=jnp.float32)
+        second = jnp.dot(block, gate_buf[slot, 1], preferred_element_type=jnp.float32)
+        pre_mine[i] = jnp.concatenate([first[:slots], second[slots:]], axis=0).astype(
+            jnp.bfloat16
+        )
+
+        @pl.when(lax.rem(i, tensor_count) < tensor_count - 1)
+        def _():
+            pre_copy(i).start()
+
+        @pl.when(i + gate_slots < pairs)
+        def _():
+            gate_copy(i + gate_slots).start()
+
+        @pl.when(i == 0)
+        def _():
+            for copy in square_sends:
+                copy.wait_recv()
+            mean_square = square_sum[0]
+            for s in range(1, tensor_count):
+                mean_square = mean_square + square_sum[s]
+            scale = lax.rsqrt(mean_square / (width * tensor_count) + 1e-06)
+            slot_scale[...] = jnp.dot(
+                placing,
+                scale,
+                precision=lax.Precision.HIGHEST,
+                preferred_element_type=jnp.float32,
+            )
+
+        @pl.when((i - lag >= tensor_count - 1) & (lax.rem(i - lag, tensor_count) == tensor_count - 1))
+        def _():
+            reduce_pair((i - lag) // tensor_count)
+
+        return carry
+
+    lax.fori_loop(0, pairs, gate_step, 0)
+    reduce_pair(per_owner - 1)
+
+    def down_step(i, carry):
+        pair = down_pair(i)
+        slot = lax.rem(i, down_slots)
+        d, k = lax.rem(i, tensor_count), i // tensor_count
+
+        @pl.when(d > 0)
+        def _():
+            pltpu.make_async_remote_copy(
+                src_ref=hidden_all.at[pair],
+                dst_ref=hidden_all.at[pair],
+                send_sem=hid_send.at[k, tensor_count - d - 1],
+                recv_sem=hid_recv.at[k, tensor_count - d - 1],
+                device_id={"tensor": t_at(d)},
+                device_id_type=pl.DeviceIdType.MESH,
+            ).wait_recv()
+
+        down_copy(i).wait()
+        block = hidden_all[pair]
+        first = jnp.dot(block, down_buf[slot, 0], preferred_element_type=jnp.float32)
+        second = jnp.dot(block, down_buf[slot, 1], preferred_element_type=jnp.float32)
+        result_all[pl.ds(pl.multiple_of(pair * 2 * slots, 2 * slots), 2 * slots), :] = (
+            jnp.concatenate([first[:slots], second[slots:]], axis=0).astype(jnp.bfloat16)
+        )
+
+        @pl.when(i + down_slots < pairs)
+        def _():
+            down_copy(i + down_slots).start()
+
+        return carry
+
+    lax.fori_loop(0, pairs, down_step, 0)
+
+    both = jnp.dot(
+        jnp.concatenate([gate_high, gate_low], axis=0),
+        result_all[...],
+        preferred_element_type=jnp.float32,
+    )
+    mixture = both[:all_rows] + both[all_rows:]
+    for b in range(owner_count):
+        mix_mine[b] = mixture[b * rows : (b + 1) * rows]
+    mix_sends = [
+        remote("expert", d, 7, mix_mine.at[e_at(d)], mix_got.at[d - 1]) for d in e_offsets
+    ]
+    for copy in mix_sends:
+        copy.start()
+    for copy in mix_sends:
+        copy.wait_recv()
+    total = wide + mix_mine[e_me]
+    for d in e_offsets:
+        total = total + mix_got[d - 1]
+    out_ref[...] = total.astype(jnp.bfloat16)
+
+    for copy in info_sends + part_sends + term_sends + row_sends + square_sends + mix_sends:
+        copy.wait_send()
+    for k in range(per_owner):
+        for d in range(tensor_count - 1):
+            pre_copy(k * tensor_count + d).wait_send()
+            hid_copy(k, d + 1).wait_send()
+
+
+def fits_kernel(shapes, tensor_count, owner_count):
+    queries, keys, gate_up, down_proj = shapes
+    rows = queries[0]
+    head_count = queries[1] // HD
+    experts = gate_up[0]
+    return (
+        tensor_count == KV
+        and rows == 8
+        and head_count == 8 * KV
+        and owner_count * MOST == 8
+        and experts * owner_count * MOST == 128
+        and experts % (2 * tensor_count) == 0
+        and gate_up[1] % 256 == 0
+        and down_proj[1] % 128 == 0
+        and keys[1] % 128 == 0
+    )
+
+
+def fused(
+    hidden_in,
+    queries,
+    cache_keys,
+    cache_values,
+    new_key,
+    new_value,
+    cache_lengths,
+    out_weight,
+    norm_gain,
+    gate_probs,
+    expert_ids,
+    gate_up,
+    down_proj,
+):
+    tensor_count = lax.axis_size("tensor")
+    owner_count = lax.axis_size("expert")
+    rows, width = hidden_in.shape
+    group_size = queries.shape[1] // HD // KV
+    experts, units = gate_up.shape[0], down_proj.shape[1]
+    pairs = experts // 2
+    per_owner = pairs // tensor_count
+    slots = owner_count * MOST
+    heads = rows * group_size
+    half = width // 2
+    vmem = pl.BlockSpec(memory_space=pltpu.VMEM)
+    far = pl.BlockSpec(memory_space=pl.ANY)
+    dma = pltpu.SemaphoreType.DMA
+    f32, bf16 = jnp.float32, jnp.bfloat16
+    gate_slots, down_slots = min(5, pairs), min(4, pairs)
+    others = max(tensor_count, owner_count) - 1
+    return pl.pallas_call(
+        functools.partial(fused_kernel, tensor_count, owner_count),
+        out_shape=jax.ShapeDtypeStruct((rows, width), bf16),
+        in_specs=[vmem] * 8 + [far] * 5,
+        out_specs=vmem,
+        scratch_shapes=[
+            pltpu.VMEM(cache_keys.shape, bf16),
+            pltpu.VMEM(cache_values.shape, bf16),
+            pltpu.VMEM(out_weight.shape, bf16),
+            pltpu.VMEM((gate_slots, 2) + gate_up.shape[1:], bf16),
+            pltpu.VMEM((down_slots, 2) + down_proj.shape[1:], bf16),
+            pltpu.VMEM((KV, heads, HD), f32),
+            pltpu.VMEM((KV, heads, HD), f32),
+            pltpu.VMEM((KV, heads, HD), f32),
+            pltpu.VMEM((KV + tensor_count, 8, 128), f32),
+            pltpu.VMEM((KV + tensor_count, heads, HD), bf16),
+            pltpu.VMEM((2 * tensor_count, 2 * rows, half), bf16),
+            pltpu.VMEM((owner_count, rows, 128), f32),
+            pltpu.VMEM((owner_count, 2 * rows, half), bf16),
+            pltpu.VMEM((owner_count, rows, 128), f32),
+            pltpu.VMEM((tensor_count, owner_count * rows, 128), f32),
+            pltpu.VMEM((experts * slots, width), bf16),
+            pltpu.VMEM((experts * slots, 128), f32),
+            pltpu.VMEM((pairs, 2 * slots, 2 * units), bf16),
+            pltpu.VMEM((per_owner, tensor_count - 1, 2 * slots, 2 * units), bf16),
+            pltpu.VMEM((pairs, 2 * slots, units), bf16),
+            pltpu.VMEM((experts * slots, width), bf16),
+            pltpu.VMEM((owner_count, rows, width), f32),
+            pltpu.VMEM((owner_count - 1, rows, width), f32),
+            dma((3,)),
+            dma((gate_slots,)),
+            dma((down_slots,)),
+            dma((8, others)),
+            dma((8, others)),
+            dma((per_owner, tensor_count - 1)),
+            dma((per_owner, tensor_count - 1)),
+            dma((per_owner, tensor_count - 1)),
+            dma((per_owner, tensor_count - 1)),
+        ],
+        compiler_params=pltpu.CompilerParams(
+            collective_id=0, has_side_effects=True, vmem_limit_bytes=62 * 1024 * 1024
+        ),
+    )(
+        hidden_in,
+        queries.reshape(rows, KV, group_size, HD),
+        new_key,
+        new_value,
+        jnp.broadcast_to(cache_lengths[:, None], (rows, 128)),
+        norm_gain[None, :],
+        gate_probs,
+        expert_ids,
+        cache_keys,
+        cache_values,
+        out_weight,
+        gate_up,
+        down_proj,
+    )
+
+
+def layer(*args):
+    shapes = (args[1].shape, args[2].shape, args[11].shape, args[12].shape)
+    if fits_kernel(shapes, lax.axis_size("tensor"), lax.axis_size("expert")):
+        return fused(*args)
+    return body(*args)
+
+
 def solution(mesh):
     return jax.shard_map(
-        body,
+        layer,
         mesh=mesh,
         in_specs=(
             P(("groups", "expert"), "tensor"),

time: 183 us -> 50.9 us (0.28)
  waiting for transfers between devices: 64.3 us -> 0 us
  blocking collectives: 50.7 us -> 0 us
  Pallas kernels: 0 us -> 45.2 us
  matrix products: 40.9 us -> 0 us
  between operations: 14 us -> 0.01 us
  other arithmetic: 4.21 us -> 0 us
  starting transfers between devices: 3.49 us -> 0 us
    pallas_call x0 -> x1, Pallas kernels: none -> 45.2 us  [fused(): pl.pallas_call(functools.partial(fused_kernel, tensor_count, owner_count)...]
    dot_general x8 -> x0, matrix products: 40.9 us -> none  [the longest x1 19.5 us: body(): jnp.einsum('erd,edf->erf', slot_rows, gate_up, preferred_element_type=jnp...]
    psum x1 -> x0, waiting for transfers between devices: 34.4 us -> none  [body(): lax.psum(pre_term.astype(jnp.bfloat16), 'tensor').astype(jnp.float32)]
    reduce_scatter x2 -> x0, waiting for transfers between devices: 23.8 us -> none  [the longest x1 17.3 us: body(): lax.psum_scatter(proj_term.astype(jnp.bfloat16), 'tensor', scatter_dimens...]
    pmax x1 -> x0, blocking collectives: 20.6 us -> none  [body(): global_high = lax.pmax(local_high, 'tensor')]
    all_gather x1 -> x0, blocking collectives: 13.1 us -> none  [body(): lax.all_gather(residual, 'tensor', axis=1, tiled=True).astype(jnp.float32)]
    all_to_all x1 -> x0, blocking collectives: 8.57 us -> none  [body(): lax.all_to_all(outgoing, 'expert', split_axis=1, concat_axis=1, tiled=True)]
    unnamed x1 -> x0, blocking collectives: 8.35 us -> none
  transfers between devices with their start and end apart: 4 -> 0, of which waited for: 4 -> 0; matrix products, arithmetic and copies ran while one was open for 1% -> 0% of each run, Pallas kernels for 0% -> 0%
where the time goes in v1:
time: 50.9 us; the launch traced here: 50.6 us
  Pallas kernels  45.2 us (89%)
  local copies, waits for them, and re-layouts  5.38 us (11%)
    pallas_call x1, Pallas kernels, fused(): pl.pallas_call(functools.partial(fused_kernel, tensor_count, owner_count)...  45.2 us
    unnamed x2, local copies, waits for them, and re-layouts  2.79 us
    broadcast_in_dim x1, local copies, waits for them, and re-layouts, fused(): jnp.broadcast_to(cache_lengths[:, None], (rows, 128))  1.31 us
    broadcast_in_dim x1, local copies, waits for them, and re-layouts, fused(): norm_gain[None, :]  1.28 us

profile of v1, /device:TPU:0, one launch (start us, length us, event | category | flops | bytes accessed | tf_op | source)
XLA Modules:
  0.0 50.6 jit_solution(16158389778430045733)
XLA Ops:
  0.0 1.3 %broadcast_in_dim.4.length_ref = s32[8,128]{1,0:T(8,128)} broadcast(s32[8]{0:T(128)} %param.19), dimensions={0} | broadcast | bytes 4128 | tf_op jit(solution)/shard_map/broadcast_in_dim | solution.py:734
  1.3 1.3 %broadcast_in_dim.10.gain_ref = bf16[1,1024]{1,0:T(2,128)(2,1)} reshape(bf16[1024]{0:T(1024)(128)(2,1)} %param.21) | data formatting | bytes 4096 | tf_op jit(solution)/shard_map/broadcast_in_dim | solution.py:735
  2.6 1.5 %copy.16 = bf16[1,8,32,128]{3,2,1,0:T(8,128)(2,1)} copy(bf16[1,8,32,128]{3,1,2,0:T(8,128)(2,1)} %bitcast.6) | data formatting | bytes 131072
  4.1 45.2 %shard_map.127 = bf16[8,1024]{1,0:T(8,128)(2,1)} custom-call(bf16[8,1024]{1,0:T(8,128)(2,1)} %hidden_ref.1, bf16[8,4,8,128]{3,2,1,0:T(8,128)(2,1)} %bitcast.5, bf16[8,512]{1,0:T(8,128)(2,1)} %new_key_ref.1, bf16[8,512]{1,0:T(8,128)(2,1)} %new_value_ref.1, s32[8,128]{1,0:T(8,128)} %broadcast_in_dim.4.length_ref, bf16[1,1024]{1,0:T(2,128)(2,1)} %broadcast_in_dim.10.gain_ref, ...), custom_call_target="tpu_custom_call" | custom-call | tf_op jit(solution)/shard_map/pallas_call | solution.py:687
  49.3 1.3 %copy.18 = bf16[8,1024]{1,0:T(8,128)(2,1)} copy(bf16[8,1024]{1,0:T(8,128)(2,1)} %shard_map.127) | data formatting | bytes 32768

commit v2 on v1

--- a/solution.py
+++ b/solution.py
@@ -173,6 +173,7 @@
     proj_buf,
     gate_buf,
     down_buf,
+    query_heads,
     part_high,
     part_total,
     part_value,
@@ -202,7 +203,9 @@
     hid_recv,
 ):
     rows, width = hidden_ref.shape
-    kv_count, group_size = query_ref.shape[1], query_ref.shape[2]
+    kv_count = KV
+    head_count = query_ref.shape[1] // HD
+    group_size = head_count // KV
     local_length = key_hbm.shape[1]
     units = down_hbm.shape[1]
     experts = gate_hbm.shape[0]
@@ -283,6 +286,11 @@
         earlier = earlier + jnp.where(row > j, count[j : j + 1, :], 0.0)
     info_all[e_me] = jnp.where(earlier == (lane % MOST).astype(jnp.float32), named, 0.0)
 
+    for h in range(head_count):
+        query_heads[h * rows : (h + 1) * rows, :] = query_ref[:, h * HD : (h + 1) * HD].astype(
+            jnp.float32
+        )
+
     key_copy.wait()
     value_copy.wait()
     for i in range(gate_slots):
@@ -299,11 +307,12 @@
         jnp.int32, (kv_count * group_size, local_length), 1
     )
     for r in range(rows):
-        live = position < length_ref[r : r + 1, 0:1]
+        live = position < length_ref[r]
+        query = query_heads[pl.ds(r, head_count, stride=rows), :].astype(jnp.bfloat16)
         scores = jnp.concatenate(
             [
                 lax.dot_general(
-                    query_ref[r, v],
+                    query[v * group_size : (v + 1) * group_size],
                     key_buf[r, :, v * HD : (v + 1) * HD],
                     (((1,), (1,)), ((), ())),
                     preferred_element_type=jnp.float32,
@@ -357,7 +366,13 @@
         wide_block = jnp.broadcast_to(block[:, None, :], (rows, group_size, HD))
         return wide_block.reshape(heads, HD)
 
-    my_query = query_ref[:, t_me].astype(jnp.float32).reshape(heads, HD)
+    my_query = jnp.concatenate(
+        [
+            query_heads[pl.ds(t_me * heads + r, group_size, stride=rows), :]
+            for r in range(rows)
+        ],
+        axis=0,
+    )
     own_score = jnp.sum(my_query * spread(own_key), axis=1, keepdims=True) * score_scale
     for copy in part_sends:
         copy.wait_recv()
@@ -432,7 +447,7 @@
         proj_sum = proj_sum + unstack(term_all[s])
     residual = (hidden_ref[...].astype(jnp.float32) + proj_sum).astype(jnp.bfloat16)
     wide = residual.astype(jnp.float32)
-    rows_all[e_me] = stack(wide * gain_ref[...].astype(jnp.float32))
+    rows_all[e_me] = stack(wide * gain_ref[...].astype(jnp.float32).reshape(1, width))
     square_all[e_me] = jnp.broadcast_to(
         jnp.sum(wide * wide, axis=1, keepdims=True), (rows, 128)
     )
@@ -687,7 +702,10 @@
     return pl.pallas_call(
         functools.partial(fused_kernel, tensor_count, owner_count),
         out_shape=jax.ShapeDtypeStruct((rows, width), bf16),
-        in_specs=[vmem] * 8 + [far] * 5,
+        in_specs=[vmem] * 4
+        + [pl.BlockSpec(memory_space=pltpu.SMEM)]
+        + [vmem] * 3
+        + [far] * 5,
         out_specs=vmem,
         scratch_shapes=[
             pltpu.VMEM(cache_keys.shape, bf16),
@@ -695,6 +713,7 @@
             pltpu.VMEM(out_weight.shape, bf16),
             pltpu.VMEM((gate_slots, 2) + gate_up.shape[1:], bf16),
             pltpu.VMEM((down_slots, 2) + down_proj.shape[1:], bf16),
+            pltpu.VMEM((KV * heads, HD), f32),
             pltpu.VMEM((KV, heads, HD), f32),
             pltpu.VMEM((KV, heads, HD), f32),
             pltpu.VMEM((KV, heads, HD), f32),
@@ -728,11 +747,11 @@
         ),
     )(
         hidden_in,
-        queries.reshape(rows, KV, group_size, HD),
+        queries,
         new_key,
         new_value,
-        jnp.broadcast_to(cache_lengths[:, None], (rows, 128)),
-        norm_gain[None, :],
+        cache_lengths,
+        norm_gain,
         gate_probs,
         expert_ids,
         cache_keys,

time: 50.9 us -> 46.8 us (0.919)
  local copies, waits for them, and re-layouts: 5.38 us -> 1.32 us
    broadcast_in_dim x2 -> x0, local copies, waits for them, and re-layouts: 2.59 us -> none  [the longest x1 1.31 us: fused(): jnp.broadcast_to(cache_lengths[:, None], (rows, 128))]
    unnamed x2 -> x1, local copies, waits for them, and re-layouts: 2.79 us -> 1.32 us
where the time goes in v2:
time: 46.8 us; the launch traced here: 46.5 us
  Pallas kernels  45.2 us (97%)
  local copies, waits for them, and re-layouts  1.32 us (3%)
    pallas_call x1, Pallas kernels, fused(): pl.pallas_call(functools.partial(fused_kernel, tensor_count, owner_count)...  45.2 us
    unnamed x1, local copies, waits for them, and re-layouts  1.32 us

profile of v2, /device:TPU:0, one launch (start us, length us, event | category | flops | bytes accessed | tf_op | source)
XLA Modules:
  0.0 46.5 jit_solution(13402243213377947296)
XLA Ops:
  0.0 45.2 %shard_map.127 = bf16[8,1024]{1,0:T(8,128)(2,1)} custom-call(bf16[8,1024]{1,0:T(8,128)(2,1)} %hidden_ref.1, bf16[8,4096]{1,0:T(8,128)(2,1)} %query_ref.1, bf16[8,512]{1,0:T(8,128)(2,1)} %new_key_ref.1, bf16[8,512]{1,0:T(8,128)(2,1)} %new_value_ref.1, s32[8]{0:T(128)} %length_ref.1, bf16[1024]{0:T(1024)(128)(2,1)} %gain_ref.1, f32[8,8]{1,0:T(8,128)} %prob_ref.1, ...), custom_call_target="tpu_custom_call" | custom-call | tf_op jit(solution)/shard_map/pallas_call | solution.py:702
  45.2 1.3 %copy.15 = bf16[8,1024]{1,0:T(8,128)(2,1)} copy(bf16[8,1024]{1,0:T(8,128)(2,1)} %shard_map.127) | data formatting | bytes 32768

commit v3 on v2

--- a/solution.py
+++ b/solution.py
@@ -261,7 +261,6 @@
     proj_copy = pltpu.make_async_copy(proj_hbm, proj_buf, load_sem.at[2])
     key_copy.start()
     value_copy.start()
-    proj_copy.start()
 
     barrier = pltpu.get_barrier_semaphore()
     for d in t_offsets:
@@ -293,6 +292,7 @@
 
     key_copy.wait()
     value_copy.wait()
+    proj_copy.start()
     for i in range(gate_slots):
         gate_copy(i).start()
     for i in range(down_slots):
@@ -448,8 +448,8 @@
     residual = (hidden_ref[...].astype(jnp.float32) + proj_sum).astype(jnp.bfloat16)
     wide = residual.astype(jnp.float32)
     rows_all[e_me] = stack(wide * gain_ref[...].astype(jnp.float32).reshape(1, width))
-    square_all[e_me] = jnp.broadcast_to(
-        jnp.sum(wide * wide, axis=1, keepdims=True), (rows, 128)
+    square_all[e_me] = jnp.where(
+        lane == e_me * rows + row, jnp.sum(wide * wide, axis=1, keepdims=True), 0.0
     )
     row_sends = []
     for d in e_offsets:
@@ -502,7 +502,10 @@
         gathered.astype(jnp.bfloat16),
         preferred_element_type=jnp.float32,
     ).astype(jnp.bfloat16)
-    square_sum[t_me] = jnp.concatenate([square_all[b] for b in range(owner_count)], axis=0)
+    squares = square_all[0]
+    for b in range(1, owner_count):
+        squares = squares + square_all[b]
+    square_sum[t_me] = squares
     square_sends = [
         remote("tensor", d, 6, square_sum.at[t_me], square_sum.at[t_me]) for d in t_offsets
     ]
@@ -545,7 +548,19 @@
         for d in t_offsets:
             hid_copy(k, d).start()
 
-    lag = 2
+    lag = 3
+
+    def scale_slots():
+        for copy in square_sends:
+            copy.wait_recv()
+        squares = square_sum[0]
+        for s in range(1, tensor_count):
+            squares = squares + square_sum[s]
+        mean_square = jnp.sum(squares, axis=0, keepdims=True) / (width * tensor_count)
+        scale = lax.rsqrt(mean_square + 1e-06)
+        slot_scale[...] = jnp.broadcast_to(
+            jnp.sum(placing * scale[:, :all_rows], axis=1, keepdims=True), (slot_total, 128)
+        )
 
     def gate_step(i, carry):
         pair = gate_pair(i)
@@ -566,20 +581,9 @@
         def _():
             gate_copy(i + gate_slots).start()
 
-        @pl.when(i == 0)
+        @pl.when(i == lag)
         def _():
-            for copy in square_sends:
-                copy.wait_recv()
-            mean_square = square_sum[0]
-            for s in range(1, tensor_count):
-                mean_square = mean_square + square_sum[s]
-            scale = lax.rsqrt(mean_square / (width * tensor_count) + 1e-06)
-            slot_scale[...] = jnp.dot(
-                placing,
-                scale,
-                precision=lax.Precision.HIGHEST,
-                preferred_element_type=jnp.float32,
-            )
+            scale_slots()
 
         @pl.when((i - lag >= tensor_count - 1) & (lax.rem(i - lag, tensor_count) == tensor_count - 1))
         def _():
@@ -588,7 +592,6 @@
         return carry
 
     lax.fori_loop(0, pairs, gate_step, 0)
-    reduce_pair(per_owner - 1)
 
     def down_step(i, carry):
         pair = down_pair(i)
@@ -620,7 +623,10 @@
 
         return carry
 
-    lax.fori_loop(0, pairs, down_step, 0)
+    last = (per_owner - 1) * tensor_count
+    lax.fori_loop(0, last, down_step, 0)
+    reduce_pair(per_owner - 1)
+    lax.fori_loop(last, pairs, down_step, 0)
 
     both = jnp.dot(
         jnp.concatenate([gate_high, gate_low], axis=0),
@@ -629,7 +635,7 @@
     )
     mixture = both[:all_rows] + both[all_rows:]
     for b in range(owner_count):
-        mix_mine[b] = mixture[b * rows : (b + 1) * rows]
+        mix_mine[b] = stack(mixture[b * rows : (b + 1) * rows])
     mix_sends = [
         remote("expert", d, 7, mix_mine.at[e_at(d)], mix_got.at[d - 1]) for d in e_offsets
     ]
@@ -637,9 +643,9 @@
         copy.start()
     for copy in mix_sends:
         copy.wait_recv()
-    total = wide + mix_mine[e_me]
+    total = wide + unstack(mix_mine[e_me])
     for d in e_offsets:
-        total = total + mix_got[d - 1]
+        total = total + unstack(mix_got[d - 1])
     out_ref[...] = total.astype(jnp.bfloat16)
 
     for copy in info_sends + part_sends + term_sends + row_sends + square_sends + mix_sends:
@@ -723,15 +729,15 @@
             pltpu.VMEM((owner_count, rows, 128), f32),
             pltpu.VMEM((owner_count, 2 * rows, half), bf16),
             pltpu.VMEM((owner_count, rows, 128), f32),
-            pltpu.VMEM((tensor_count, owner_count * rows, 128), f32),
+            pltpu.VMEM((tensor_count, rows, 128), f32),
             pltpu.VMEM((experts * slots, width), bf16),
             pltpu.VMEM((experts * slots, 128), f32),
             pltpu.VMEM((pairs, 2 * slots, 2 * units), bf16),
             pltpu.VMEM((per_owner, tensor_count - 1, 2 * slots, 2 * units), bf16),
             pltpu.VMEM((pairs, 2 * slots, units), bf16),
             pltpu.VMEM((experts * slots, width), bf16),
-            pltpu.VMEM((owner_count, rows, width), f32),
-            pltpu.VMEM((owner_count - 1, rows, width), f32),
+            pltpu.VMEM((owner_count, 2 * rows, half), bf16),
+            pltpu.VMEM((owner_count - 1, 2 * rows, half), bf16),
             dma((3,)),
             dma((gate_slots,)),
             dma((down_slots,)),

time: 46.8 us -> 52.1 us (1.11)
  Pallas kernels: 45.2 us -> 50.5 us
    pallas_call x1, Pallas kernels: 45.2 us -> 50.5 us  [fused(): pl.pallas_call(functools.partial(fused_kernel, tensor_count, owner_count)...]
where the time goes in v3:
time: 52.1 us; the launch traced here: 51.9 us
  Pallas kernels  50.5 us (97%)
  local copies, waits for them, and re-layouts  1.32 us (3%)
    pallas_call x1, Pallas kernels, fused(): pl.pallas_call(functools.partial(fused_kernel, tensor_count, owner_count)...  50.5 us
    unnamed x1, local copies, waits for them, and re-layouts  1.32 us

profile of v3, /device:TPU:0, one launch (start us, length us, event | category | flops | bytes accessed | tf_op | source)
XLA Modules:
  0.0 51.9 jit_solution(13281378409751952763)
XLA Ops:
  0.0 50.5 %shard_map.127 = bf16[8,1024]{1,0:T(8,128)(2,1)} custom-call(bf16[8,1024]{1,0:T(8,128)(2,1)} %hidden_ref.1, bf16[8,4096]{1,0:T(8,128)(2,1)} %query_ref.1, bf16[8,512]{1,0:T(8,128)(2,1)} %new_key_ref.1, bf16[8,512]{1,0:T(8,128)(2,1)} %new_value_ref.1, s32[8]{0:T(128)} %length_ref.1, bf16[1024]{0:T(1024)(128)(2,1)} %gain_ref.1, f32[8,8]{1,0:T(8,128)} %prob_ref.1, ...), custom_call_target="tpu_custom_call" | custom-call | tf_op jit(solution)/shard_map/pallas_call | solution.py:708
  50.5 1.3 %copy.15 = bf16[8,1024]{1,0:T(8,128)(2,1)} copy(bf16[8,1024]{1,0:T(8,128)(2,1)} %shard_map.127) | data formatting | bytes 32768
